TPU v7x, 32 devices: a whole 2x2x4 slice. The times are simulated.
32 devices in a mesh: grid: 16 (over z, x, core), rep: 2 (over y).
Axes of the slice: x: 2, y: 2, z: 4, core: 2. Of those that a mesh axis runs over, the one named last changes fastest.
Arguments:
- density: bfloat16 [1280, 1280], P('grid', 'rep'), may hold values from -0.625 to 0.625
- density_pattern: int32 [10, 10], replicated, may hold values 0 or 1
- square_pattern: int32 [10, 10], replicated, may hold values 0 or 1
- cube_pattern: int32 [10, 10], replicated, may hold values 0 or 1
- block_order: int32 [10], replicated, may hold values from 0 to 9, each once
Outputs:
- purified: float32 [1280, 1280], P('grid', 'rep')
All inputs are finite; a program needn't handle non-finite values.
Results may differ from a plain program's by a relative error of at most 0.0025.
Values may be sent and summed in bfloat16 or wider, within the bound.
No kernel may reach another device: no remote copies, remote signals or barrier semaphores. Data moves between devices by JAX's collectives and lax.ppermute only.
A program may use at most 64 MiB of HBM per device.

v0:
```python
import functools
import math

import jax
import jax.numpy as jnp
from jax import lax
from jax.experimental import pallas as pl
from jax.experimental.pallas import tpu as pltpu
from jax.sharding import PartitionSpec as P

BLOCK = 128
TILE = 16
PLACE = 10**9
IN_SMEM = pl.BlockSpec(memory_space=pltpu.SMEM)
IN_VMEM = pl.BlockSpec(memory_space=pltpu.VMEM)


def factors(size):
    pair = 2 if size % 2 == 0 else 1
    rest = size // pair
    outer = 4 if rest % 4 == 0 else 1
    return outer, rest // outer, pair


def send(value, dims, axis, step):
    outer, inner, pair = dims
    pairs = []
    for source in range(outer * inner * pair):
        place = [source // (inner * pair), source // pair % inner, source % pair]
        place[axis] = (place[axis] + step) % dims[axis]
        pairs.append((source, (place[0] * inner + place[1]) * pair + place[2]))
    return lax.ppermute(value, "grid", pairs)


def source_row(piece, dims, rows):
    outer, inner, pair = dims
    here = lax.axis_index("grid")
    at = (here // (inner * pair), here // pair % inner, here % pair)
    z, x, c = [lax.rem(a - k + d, d) for a, k, d in zip(at, piece[:3], dims)]
    return pl.multiple_of(((z * inner + x) * pair + c) * rows + piece[3], TILE)


def after(value, *others):
    return lax.optimization_barrier((value,) + others)[0]


def pick(pattern, order, row_block, col_block):
    return pattern[order[row_block], order[col_block]].astype(jnp.float32)


def rows_mask(pattern, order, first_row, rows, first_col_block, col_blocks):
    top = first_row // BLOCK
    low = (first_row + rows - 1) // BLOCK
    split = (top + 1) * BLOCK - first_row
    upper = lax.broadcasted_iota(jnp.int32, (rows, BLOCK), 0) < split
    tiles = []
    for j in range(col_blocks):
        a = pick(pattern, order, top, first_col_block + j)
        b = pick(pattern, order, low, first_col_block + j)
        tiles.append(jnp.where(upper, a, b))
    return jnp.concatenate(tiles, axis=1)


def parts_of(packed):
    count = packed.shape[1]
    patterns = [packed.at[pl.ds(at * count, count), :] for at in range(3)]
    return (*patterns, packed.at[3 * count])


def prepare_kernel(reps, packed, table, panel_keep, square_keep, cube_keep):
    density_pattern, square_pattern, cube_pattern, order = parts_of(packed)
    here, rep = lax.axis_index("grid"), lax.axis_index("rep")
    row_blocks, _, cols = table.shape
    rows = square_keep.shape[0]
    col_blocks = cols // BLOCK
    first_col = rep * col_blocks

    def fill(i, _):
        for j in range(col_blocks):
            keep = pick(density_pattern, order, i, first_col + j)
            tile = jnp.full((TILE, BLOCK), keep, jnp.float32).astype(jnp.bfloat16)
            table[i, :, j * BLOCK:(j + 1) * BLOCK] = tile
        return 0

    lax.fori_loop(0, row_blocks, fill, 0, unroll=row_blocks <= 16)
    for q in range(reps):
        at = lax.rem(rep - q + reps, reps) * col_blocks
        keep = rows_mask(density_pattern, order, here * rows, rows, at, col_blocks)
        panel_keep[q] = keep.astype(jnp.bfloat16)
    for pattern, keep in ((square_pattern, square_keep), (cube_pattern, cube_keep)):
        keep[...] = rows_mask(pattern, order, here * rows, rows, first_col, col_blocks)


def panel_kernel(reps, panel_keep, *refs):
    panel, (left, own) = refs[:reps], refs[reps:]
    rep = lax.axis_index("rep")
    cols = panel[0].shape[1]
    for q in range(reps):
        at = pl.multiple_of(lax.rem(rep - q + reps, reps) * cols, BLOCK)
        part = panel[q][...] * panel_keep[q]
        left[:, pl.ds(at, cols)] = part
        if q == 0:
            own[...] = part


def masked_tile(source, at, table, stored_row):
    return source[at:at + TILE, :] * table[stored_row // BLOCK]


def stack_kernel(*refs):
    out, done = refs[-1], 0
    for ref in refs[:-1]:
        out[done:done + ref.shape[0], :] = ref[...]
        done += ref.shape[0]


def early_kernel(groups, late, dims, left, table, *refs):
    held, (band, partial) = refs[:len(groups)], refs[len(groups):]
    rows, cols = partial.shape
    for pieces, ref in zip(groups, held):
        done = 0
        for piece in pieces:
            row = source_row(piece, dims, rows)
            for at in range(0, piece[4] - piece[3], TILE):
                tile = masked_tile(ref, done, table, row + at)
                band[pl.ds(pl.multiple_of(row + at, TILE), TILE), :] = tile
                done += TILE
    for piece in late:
        count = piece[4] - piece[3]
        band[pl.ds(source_row(piece, dims, rows), count), :] = jnp.zeros((count, cols), band.dtype)
    partial[...] = jnp.dot(left[...], band[...], preferred_element_type=jnp.float32)


def late_kernel(late, dims, table, square_keep, left, old_band, partial, *refs):
    pieces, (band, tripled, square_half, window) = refs[:len(late)], refs[len(late):]
    rows, cols = partial.shape
    pair = dims[2]
    total = partial[...]
    for first in range(0, len(late), pair):
        base = late[first]
        start = source_row(base, dims, rows)
        start = start - lax.rem(start, rows * pair)
        low = jnp.minimum(start // BLOCK * BLOCK, band.shape[0] - window.shape[0])
        low = pl.multiple_of(low, BLOCK)
        window[...] = jnp.zeros(window.shape, window.dtype)
        for piece, ref in zip(late[first:first + pair], pieces[first:first + pair]):
            row = source_row(piece, dims, rows)
            for at in range(0, ref.shape[0], TILE):
                tile = masked_tile(ref, at, table, row + at)
                window[pl.ds(pl.multiple_of(row + at - low, TILE), TILE), :] = tile
                band[pl.ds(pl.multiple_of(row + at, TILE), TILE), :] = tile
        total += jnp.dot(
            left[:, pl.ds(low, window.shape[0])], window[...], preferred_element_type=jnp.float32
        )
    total *= square_keep[...]
    tripled[...] = 3.0 * total
    square_half[...] = total.astype(jnp.bfloat16)


def cube_kernel(shift, keep, half, band, before, out):
    rep, reps = lax.axis_index("rep"), lax.axis_size("rep")
    cols = before.shape[1]
    at = lax.rem(rep - shift + reps, reps)
    right = band[pl.ds(pl.multiple_of(at * cols, BLOCK), cols), :]
    part = jnp.dot(half[...], right, preferred_element_type=jnp.float32)
    out[...] = before[...] - 2.0 * (part * keep[...])


def shifted(own, reps):
    return [
        lax.ppermute(own, "rep", [(s, (s + q) % reps) for s in range(reps)])
        for q in range(1, reps)
    ]


def on_device(grid, reps, density, density_pattern, square_pattern, cube_pattern, block_order):
    rows, cols = density.shape
    order = grid * rows
    dims = factors(grid)
    outer, inner, pair = dims
    band_bytes = order * cols * 2
    room = min(3 * band_bytes + (4 << 20), 56 << 20)
    bf16, f32 = jnp.bfloat16, jnp.float32

    def call(kernel, name, flops, moved, out, operands, spec=None, **more):
        return pl.pallas_call(
            kernel,
            out_shape=[jax.ShapeDtypeStruct(shape, dtype) for shape, dtype in out],
            in_specs=spec or [IN_VMEM] * len(operands),
            out_specs=[IN_VMEM] * len(out),
            compiler_params=pltpu.CompilerParams(vmem_limit_bytes=room),
            cost_estimate=pl.CostEstimate(flops=flops, bytes_accessed=moved, transcendentals=0),
            name=name,
            **more,
        )(*operands)

    steps, hops = list(range(1, outer)), list(range(1, inner))
    last = outer // 2 if steps and hops else None
    before = [step for step in steps if step != last][-1:]

    held = {(0, 0): density}
    for step in steps:
        held[step, 0] = send(after(density), dims, 0, step)
    for hop in hops:
        held[0, hop] = send(after(density), dims, 1, hop)
    packed = jnp.concatenate(
        [density_pattern, square_pattern, cube_pattern, after(block_order)[None]], axis=0
    )
    table, panel_keep, square_keep, cube_keep = call(
        functools.partial(prepare_kernel, reps), "prepare", PLACE, 2 * band_bytes,
        [((order // BLOCK, TILE, cols), bf16), ((reps, rows, cols), bf16),
         ((rows, cols), f32), ((rows, cols), f32)],
        [packed], spec=[IN_SMEM],
    )
    for step in steps:
        for hop in hops:
            ready = [table] if step == last else []
            held[step, hop] = send(after(held[step, 0], *ready), dims, 1, hop)
    panel = shifted(after(density), reps)
    left, own = call(
        functools.partial(panel_kernel, reps), "panel", 4 * PLACE, 2 * band_bytes,
        [((rows, reps * cols), bf16), ((rows, cols), bf16)],
        [panel_keep, after(density), *panel],
    )

    lone = [(0, 0)] + [key for key in held if key[0] == last]
    lone += [key for key in held if key[0] in before and key[1]]
    stack = [key for key in held if key not in lone]
    whole = lambda key, core: (*key, core, 0, rows)
    early, late = [], []
    for key in lone:
        group = late if key[0] == last and key[1] else early
        group.append(([whole(key, 0)], held[key] if key != (0, 0) else own))
        if pair > 1:
            value = after(held[key], *([] if group is late else [left]))
            group.append(([whole(key, 1)], send(value, dims, 2, 1)))
    early += [([whole(key, 0)], held[key]) for key in stack]
    if pair > 1 and stack:
        ready = panel + ([held[last, 0]] if hops else [])
        (stacked,) = call(
            stack_kernel, "stack", 0, 0, [((len(stack) * rows, cols), bf16)],
            [after(held[key], *ready) for key in stack],
        )
        early.append(([whole(key, 1) for key in stack], send(after(stacked), dims, 2, 1)))
    late_pieces, late_values = [piece[0] for piece, _ in late], [value for _, value in late]

    band, partial = call(
        functools.partial(early_kernel, [pieces for pieces, _ in early], late_pieces, dims),
        "square_early", 2 * rows * order * cols, 2 * band_bytes,
        [((order, cols), bf16), ((rows, cols), f32)],
        [left, table, *[value for _, value in early]],
    )
    span = BLOCK - math.gcd(pair * rows, BLOCK) + pair * rows
    span = min((span + BLOCK - 1) // BLOCK * BLOCK, order)
    band, tripled, square_half = call(
        functools.partial(late_kernel, late_pieces, dims), "square_late",
        2 * rows * span * cols, 4 * rows * cols,
        [((order, cols), bf16), ((rows, cols), f32), ((rows, cols), bf16)],
        [table, square_keep, left, band, partial, *late_values],
        input_output_aliases={3: 0},
        scratch_shapes=[pltpu.VMEM((span, cols), bf16)],
    )
    out = tripled
    for shift, half in enumerate([square_half] + shifted(square_half, reps)):
        (out,) = call(
            functools.partial(cube_kernel, shift), "cube_part",
            2 * rows * cols * cols, band_bytes // reps, [((rows, cols), f32)],
            [cube_keep, half, band, out],
        )
    return out


def solution(mesh):
    placed = (P("grid", "rep"), P(), P(), P(), P())
    return jax.shard_map(
        functools.partial(on_device, mesh.shape["grid"], mesh.shape["rep"]),
        mesh=mesh, in_specs=placed, out_specs=P("grid", "rep"), check_vma=False,
    )
```

profile of v0, /device:TPU:0, one launch (start us, length us, event | category | flops | bytes accessed | tf_op | source)
XLA Modules:
  0.0 27.0 jit_solution(8840666548002065431)
XLA Ops:
  0.0 3.0 %collective-permute-start.7 = (bf16[80,640]{1,0:T(8,128)(2,1)}, bf16[80,640]{1,0:T(8,128)(2,1)S(1)}, u32[]{:S(2)}, u32[]{:S(2)}) collective-permute-start(bf16[80,640]{1,0:T(8,128)(2,1)} %refs_0_), channel_id=1, source_target_pairs={{0,8},{2,10},{4,12},{6,14},{8,16},{10,18},{12,20},{14,22},{16,24},... | collective-permute-start | bytes 307208 | tf_op jit(solution)/shard_map/ppermute | solution.py:32
  3.0 1.5 %collective-permute-start.8 = (bf16[80,640]{1,0:T(8,128)(2,1)}, bf16[80,640]{1,0:T(8,128)(2,1)S(1)}, u32[]{:S(2)}, u32[]{:S(2)}) collective-permute-start(bf16[80,640]{1,0:T(8,128)(2,1)} %refs_0_), channel_id=1, source_target_pairs={{0,4},{2,6},{4,0},{6,2},{8,12},{10,14},{12,8},{14,10},{16,20},{18,... | collective-permute-start | bytes 307208 | tf_op jit(solution)/shard_map/ppermute | solution.py:32
  4.5 2.2 %collective-permute-start.4 = (bf16[80,640]{1,0:T(8,128)(2,1)}, bf16[80,640]{1,0:T(8,128)(2,1)S(1)}, u32[]{:S(2)}, u32[]{:S(2)}) collective-permute-start(bf16[80,640]{1,0:T(8,128)(2,1)} %refs_0_), channel_id=1, source_target_pairs={{0,24},{2,26},{4,28},{6,30},{8,0},{10,2},{12,4},{14,6},{16,8},{18,... | collective-permute-start | bytes 307208 | tf_op jit(solution)/shard_map/ppermute | solution.py:32
  6.8 0.8 %collective-permute-start.2 = (bf16[80,640]{1,0:T(8,128)(2,1)}, bf16[80,640]{1,0:T(8,128)(2,1)S(1)}, u32[]{:S(2)}, u32[]{:S(2)}) collective-permute-start(bf16[80,640]{1,0:T(8,128)(2,1)} %refs_0_), channel_id=1, source_target_pairs={{0,16},{2,18},{4,20},{6,22},{8,24},{10,26},{12,28},{14,30},{16,0},... | collective-permute-start | bytes 307208 | tf_op jit(solution)/shard_map/ppermute | solution.py:32
  7.6 1.5 %collective-permute-start = (bf16[80,640]{1,0:T(8,128)(2,1)}, bf16[80,640]{1,0:T(8,128)(2,1)S(1)}, u32[]{:S(2)}, u32[]{:S(2)}) collective-permute-start(bf16[80,640]{1,0:T(8,128)(2,1)} %refs_0_), channel_id=1, source_target_pairs={{0,1},{1,0},{2,3},{3,2},{4,5},{5,4},{6,7},{7,6},{8,9},{9,8},{10,11... | collective-permute-start | bytes 307208 | tf_op jit(solution)/shard_map/ppermute | solution.py:171
  9.1 0.0 collective-permute-done.7.refs_0_.refs_6_
  9.1 1.1 %collective-permute-start.9 = (bf16[80,640]{1,0:T(8,128)(2,1)S(1)}, bf16[80,640]{1,0:T(8,128)(2,1)S(1)}, u32[]{:S(2)}, u32[]{:S(2)}) collective-permute-start(bf16[80,640]{1,0:T(8,128)(2,1)S(1)} %collective-permute-done.7.refs_0_.refs_6_), channel_id=1, source_target_pairs={{0,4},{2,6},{4,0},{6,2},{8,12},{10,14},{12,8},{14,10},{16,20},{18,... | collective-permute-start | bytes 307208 | tf_op jit(solution)/shard_map/ppermute | solution.py:32
  10.2 0.8 %pad_add_fusion.packed = s32[31,10]{1,0:T(8,128)S(1)} fusion(s32[1,10]{1,0:T(1,128)} %bitcast.1, s32[10,10]{1,0:T(8,128)} %param.8, s32[10,10]{1,0:T(8,128)} %param.7, s32[10,10]{1,0:T(8,128)} %param.6), kind=kLoop, calls=%fused_computation | loop fusion | flops 930 | bytes 2480 | tf_op jit(solution)/shard_map/concatenate | solution.py:206
  10.9 0.0 copy-start
  10.9 1.0 %prepare.1 = (bf16[10,16,640]{2,1,0:T(8,128)(2,1)S(1)}, bf16[2,80,640]{2,1,0:T(8,128)(2,1)S(1)}, f32[80,640]{1,0:T(8,128)S(1)}, f32[80,640]{1,0:T(8,128)S(1)}) custom-call(s32[31,10]{1,0:T(8,128)S(1)} %pad_add_fusion.packed), custom_call_target="tpu_custom_call" | custom-call | flops 1000000000 | bytes 3276800 | tf_op jit(solution)/shard_map/prepare/pallas_call | solution.py:186
  12.0 0.0 collective-permute-done.4.refs_1_.refs_7_
  12.0 1.0 %collective-permute-start.5 = (bf16[80,640]{1,0:T(8,128)(2,1)S(1)}, bf16[80,640]{1,0:T(8,128)(2,1)S(1)}, u32[]{:S(2)}, u32[]{:S(2)}) collective-permute-start(bf16[80,640]{1,0:T(8,128)(2,1)S(1)} %collective-permute-done.4.refs_1_.refs_7_), channel_id=1, source_target_pairs={{0,4},{2,6},{4,0},{6,2},{8,12},{10,14},{12,8},{14,10},{16,20},{18,... | collective-permute-start | bytes 307208 | tf_op jit(solution)/shard_map/ppermute | solution.py:32
  13.0 0.0 collective-permute-done.8.refs_2_.refs_8_
  13.0 1.8 %collective-permute-done.2.refs_2_ = bf16[80,640]{1,0:T(8,128)(2,1)S(1)} collective-permute-done((bf16[80,640]{1,0:T(8,128)(2,1)}, bf16[80,640]{1,0:T(8,128)(2,1)S(1)}, u32[]{:S(2)}, u32[]{:S(2)}) %collective-permute-start.2) | collective-permute-done | bytes 102432 | tf_op jit(solution)/shard_map/ppermute | solution.py:32
  14.8 0.0 collective-permute-done.refs_1_
  14.8 1.4 %collective-permute-start.11 = (bf16[80,640]{1,0:T(8,128)(2,1)S(1)}, bf16[80,640]{1,0:T(8,128)(2,1)S(1)}, u32[]{:S(2)}, u32[]{:S(2)}) collective-permute-start(bf16[80,640]{1,0:T(8,128)(2,1)S(1)} %collective-permute-done.2.refs_2_), channel_id=1, source_target_pairs={{0,4},{2,6},{4,0},{6,2},{8,12},{10,14},{12,8},{14,10},{16,20},{18,... | collective-permute-start | bytes 307208 | tf_op jit(solution)/shard_map/ppermute | solution.py:32
  16.2 0.0 collective-permute-done.9.refs_3_.refs_9_
  16.3 0.1 collective-permute-start.10
  16.3 0.0 copy-done
  16.4 0.6 %collective-permute-start.1 = (bf16[80,640]{1,0:T(8,128)(2,1)S(1)}, bf16[80,640]{1,0:T(8,128)(2,1)S(1)}, u32[]{:S(2)}, u32[]{:S(2)}) collective-permute-start(bf16[80,640]{1,0:T(8,128)(2,1)S(1)} %copy-done), channel_id=1, source_target_pairs={{0,2},{2,0},{4,6},{6,4},{8,10},{10,8},{12,14},{14,12},{16,18},{18,... | collective-permute-start | bytes 307208 | tf_op jit(solution)/shard_map/ppermute | solution.py:32
  16.9 0.1 collective-permute-start.3
  17.0 0.0 collective-permute-done.5.refs_4_
  17.0 0.4 %collective-permute-start.6 = (bf16[80,640]{1,0:T(8,128)(2,1)S(1)}, bf16[80,640]{1,0:T(8,128)(2,1)S(1)}, u32[]{:S(2)}, u32[]{:S(2)}) collective-permute-start(bf16[80,640]{1,0:T(8,128)(2,1)S(1)} %collective-permute-done.5.refs_4_), channel_id=1, source_target_pairs={{0,2},{2,0},{4,6},{6,4},{8,10},{10,8},{12,14},{14,12},{16,18},{18,... | collective-permute-start | bytes 307208 | tf_op jit(solution)/shard_map/ppermute | solution.py:32
  17.5 2.0 %collective-permute-done.11.refs_0_ = bf16[80,640]{1,0:T(8,128)(2,1)S(1)} collective-permute-done((bf16[80,640]{1,0:T(8,128)(2,1)S(1)}, bf16[80,640]{1,0:T(8,128)(2,1)S(1)}, u32[]{:S(2)}, u32[]{:S(2)}) %collective-permute-start.11) | collective-permute-done | bytes 102432 | tf_op jit(solution)/shard_map/ppermute | solution.py:32
  19.5 0.0 collective-permute-start.12
  19.5 0.0 collective-permute-done.1.refs_1_
  19.5 0.0 collective-permute-done.3.refs_3_
  19.5 0.0 collective-permute-done.6.refs_5_
  19.5 0.0 collective-permute-done.10.refs_10_
  19.5 0.9 %square_early.1 = (bf16[1280,640]{1,0:T(8,128)(2,1)S(1)}, f32[80,640]{1,0:T(8,128)S(1)}) custom-call(bf16[80,1280]{1,0:T(8,128)(2,1)S(1)} %get-tuple-element.28.left, bf16[10,16,640]{2,1,0:T(8,128)(2,1)S(1)} %get-tuple-element.25.table, bf16[80,640]{1,0:T(8,128)(2,1)S(1)} %get-tuple-element.29.refs_0_, bf16[80,640]{1,0:T(8,128)(2,1)S(1)} %collective-permute-done.1.refs_1_, ...), custom_call_target="tpu_custom_call" | custom-call | flops 131072000 | bytes 3276800 | tf_op jit(solution)/shard_map/square_early/pallas_call | solution.py:186
  20.4 0.4 %collective-permute-done.12.refs_1_ = bf16[80,640]{1,0:T(8,128)(2,1)S(1)} collective-permute-done((bf16[80,640]{1,0:T(8,128)(2,1)S(1)}, bf16[80,640]{1,0:T(8,128)(2,1)S(1)}, u32[]{:S(2)}, u32[]{:S(2)}) %collective-permute-start.12) | collective-permute-done | bytes 102432 | tf_op jit(solution)/shard_map/ppermute | solution.py:32
  20.8 0.3 %square_late.1 = (bf16[1280,640]{1,0:T(8,128)(2,1)S(1)}, f32[80,640]{1,0:T(8,128)S(1)}, bf16[80,640]{1,0:T(8,128)(2,1)S(1)}) custom-call(bf16[10,16,640]{2,1,0:T(8,128)(2,1)S(1)} %get-tuple-element.25.table, f32[80,640]{1,0:T(8,128)S(1)} %get-tuple-element.26.square_keep, ...), custom_call_target="tpu_custom_call", output_to_operand_aliasing={{0}: (3, {})} | custom-call | flops 26214400 | bytes 204800 | tf_op jit(solution)/shard_map/square_late/pallas_call | solution.py:186
  21.1 1.6 %collective-permute-start.13 = (bf16[80,640]{1,0:T(8,128)(2,1)S(1)}, bf16[80,640]{1,0:T(8,128)(2,1)S(1)}, u32[]{:S(2)}, u32[]{:S(2)}) collective-permute-start(bf16[80,640]{1,0:T(8,128)(2,1)S(1)} %get-tuple-element.40.half), channel_id=1, source_target_pairs={{0,1},{1,0},{2,3},{3,2},{4,5},{5,4},{6,7},{7,6},{8,9},{9,8},{10,11... | collective-permute-start | bytes 307208 | tf_op jit(solution)/shard_map/ppermute | solution.py:171
  22.7 0.3 %cube_part.2.before = f32[80,640]{1,0:T(8,128)S(1)} custom-call(f32[80,640]{1,0:T(8,128)S(1)} %get-tuple-element.24.keep, bf16[80,640]{1,0:T(8,128)(2,1)S(1)} %get-tuple-element.40.half, bf16[1280,640]{1,0:T(8,128)(2,1)S(1)} %get-tuple-element.41.band, f32[80,640]{1,0:T(8,128)S(1)} %get-tuple-element.42.before), custom_call_target="tpu_custom_call" | custom-call | flops 65536000 | bytes 819200 | tf_op jit(solution)/shard_map/cube_part/pallas_call | solution.py:186
  22.9 3.1 %collective-permute-done.13.half = bf16[80,640]{1,0:T(8,128)(2,1)S(1)} collective-permute-done((bf16[80,640]{1,0:T(8,128)(2,1)S(1)}, bf16[80,640]{1,0:T(8,128)(2,1)S(1)}, u32[]{:S(2)}, u32[]{:S(2)}) %collective-permute-start.13) | collective-permute-done | bytes 102432 | tf_op jit(solution)/shard_map/ppermute | solution.py:171
  26.1 1.0 %cube_part.3 = f32[80,640]{1,0:T(8,128)} custom-call(f32[80,640]{1,0:T(8,128)S(1)} %get-tuple-element.24.keep, bf16[80,640]{1,0:T(8,128)(2,1)S(1)} %collective-permute-done.13.half, bf16[1280,640]{1,0:T(8,128)(2,1)S(1)} %get-tuple-element.41.band, f32[80,640]{1,0:T(8,128)S(1)} %cube_part.2.before), custom_call_target="tpu_custom_call" | custom-call | flops 65536000 | bytes 819200 | tf_op jit(solution)/shard_map/cube_part/pallas_call | solution.py:186
  (2 shorter events, 0.1 us)
Async XLA Ops:
  0.0 9.1 %collective-permute-start.7 = (bf16[80,640]{1,0:T(8,128)(2,1)}, bf16[80,640]{1,0:T(8,128)(2,1)S(1)}, u32[]{:S(2)}, u32[]{:S(2)}) collective-permute-start(bf16[80,640]{1,0:T(8,128)(2,1)} %refs_0_), channel_id=1, source_target_pairs={{0,8},{2,10},{4,12},{6,14},{8,16},{10,18},{12,20},{14,22},{16,24},... | collective-permute-start | bytes 307208 | tf_op jit(solution)/shard_map/ppermute | solution.py:32
  3.0 10.0 %collective-permute-start.8 = (bf16[80,640]{1,0:T(8,128)(2,1)}, bf16[80,640]{1,0:T(8,128)(2,1)S(1)}, u32[]{:S(2)}, u32[]{:S(2)}) collective-permute-start(bf16[80,640]{1,0:T(8,128)(2,1)} %refs_0_), channel_id=1, source_target_pairs={{0,4},{2,6},{4,0},{6,2},{8,12},{10,14},{12,8},{14,10},{16,20},{18,... | collective-permute-start | bytes 307208 | tf_op jit(solution)/shard_map/ppermute | solution.py:32
  4.5 7.4 %collective-permute-start.4 = (bf16[80,640]{1,0:T(8,128)(2,1)}, bf16[80,640]{1,0:T(8,128)(2,1)S(1)}, u32[]{:S(2)}, u32[]{:S(2)}) collective-permute-start(bf16[80,640]{1,0:T(8,128)(2,1)} %refs_0_), channel_id=1, source_target_pairs={{0,24},{2,26},{4,28},{6,30},{8,0},{10,2},{12,4},{14,6},{16,8},{18,... | collective-permute-start | bytes 307208 | tf_op jit(solution)/shard_map/ppermute | solution.py:32
  6.8 8.0 %collective-permute-start.2 = (bf16[80,640]{1,0:T(8,128)(2,1)}, bf16[80,640]{1,0:T(8,128)(2,1)S(1)}, u32[]{:S(2)}, u32[]{:S(2)}) collective-permute-start(bf16[80,640]{1,0:T(8,128)(2,1)} %refs_0_), channel_id=1, source_target_pairs={{0,16},{2,18},{4,20},{6,22},{8,24},{10,26},{12,28},{14,30},{16,0},... | collective-permute-start | bytes 307208 | tf_op jit(solution)/shard_map/ppermute | solution.py:32
  7.6 7.2 %collective-permute-start = (bf16[80,640]{1,0:T(8,128)(2,1)}, bf16[80,640]{1,0:T(8,128)(2,1)S(1)}, u32[]{:S(2)}, u32[]{:S(2)}) collective-permute-start(bf16[80,640]{1,0:T(8,128)(2,1)} %refs_0_), channel_id=1, source_target_pairs={{0,1},{1,0},{2,3},{3,2},{4,5},{5,4},{6,7},{7,6},{8,9},{9,8},{10,11... | collective-permute-start | bytes 307208 | tf_op jit(solution)/shard_map/ppermute | solution.py:171
  9.1 7.1 %collective-permute-start.9 = (bf16[80,640]{1,0:T(8,128)(2,1)S(1)}, bf16[80,640]{1,0:T(8,128)(2,1)S(1)}, u32[]{:S(2)}, u32[]{:S(2)}) collective-permute-start(bf16[80,640]{1,0:T(8,128)(2,1)S(1)} %collective-permute-done.7.refs_0_.refs_6_), channel_id=1, source_target_pairs={{0,4},{2,6},{4,0},{6,2},{8,12},{10,14},{12,8},{14,10},{16,20},{18,... | collective-permute-start | bytes 307208 | tf_op jit(solution)/shard_map/ppermute | solution.py:32
  10.9 5.4 %copy-start = (bf16[80,640]{1,0:T(8,128)(2,1)S(1)}, bf16[80,640]{1,0:T(8,128)(2,1)}, u32[]{:S(2)}) copy-start(bf16[80,640]{1,0:T(8,128)(2,1)} %refs_0_) | copy-start | bytes 307204
  12.0 5.1 %collective-permute-start.5 = (bf16[80,640]{1,0:T(8,128)(2,1)S(1)}, bf16[80,640]{1,0:T(8,128)(2,1)S(1)}, u32[]{:S(2)}, u32[]{:S(2)}) collective-permute-start(bf16[80,640]{1,0:T(8,128)(2,1)S(1)} %collective-permute-done.4.refs_1_.refs_7_), channel_id=1, source_target_pairs={{0,4},{2,6},{4,0},{6,2},{8,12},{10,14},{12,8},{14,10},{16,20},{18,... | collective-permute-start | bytes 307208 | tf_op jit(solution)/shard_map/ppermute | solution.py:32
  14.8 4.7 %collective-permute-start.11 = (bf16[80,640]{1,0:T(8,128)(2,1)S(1)}, bf16[80,640]{1,0:T(8,128)(2,1)S(1)}, u32[]{:S(2)}, u32[]{:S(2)}) collective-permute-start(bf16[80,640]{1,0:T(8,128)(2,1)S(1)} %collective-permute-done.2.refs_2_), channel_id=1, source_target_pairs={{0,4},{2,6},{4,0},{6,2},{8,12},{10,14},{12,8},{14,10},{16,20},{18,... | collective-permute-start | bytes 307208 | tf_op jit(solution)/shard_map/ppermute | solution.py:32
  16.3 3.2 %collective-permute-start.10 = (bf16[320,640]{1,0:T(8,128)(2,1)S(1)}, bf16[320,640]{1,0:T(8,128)(2,1)S(1)}, u32[]{:S(2)}, u32[]{:S(2)}) collective-permute-start(bf16[320,640]{1,0:T(8,128)(2,1)S(1)} %stack.1), channel_id=1, source_target_pairs={{0,2},{2,0},{4,6},{6,4},{8,10},{10,8},{12,14},{14,12},{16,18},{18,... | collective-permute-start | bytes 1228808 | tf_op jit(solution)/shard_map/ppermute | solution.py:32
  16.4 3.1 %collective-permute-start.1 = (bf16[80,640]{1,0:T(8,128)(2,1)S(1)}, bf16[80,640]{1,0:T(8,128)(2,1)S(1)}, u32[]{:S(2)}, u32[]{:S(2)}) collective-permute-start(bf16[80,640]{1,0:T(8,128)(2,1)S(1)} %copy-done), channel_id=1, source_target_pairs={{0,2},{2,0},{4,6},{6,4},{8,10},{10,8},{12,14},{14,12},{16,18},{18,... | collective-permute-start | bytes 307208 | tf_op jit(solution)/shard_map/ppermute | solution.py:32
  16.9 2.5 %collective-permute-start.3 = (bf16[80,640]{1,0:T(8,128)(2,1)S(1)}, bf16[80,640]{1,0:T(8,128)(2,1)S(1)}, u32[]{:S(2)}, u32[]{:S(2)}) collective-permute-start(bf16[80,640]{1,0:T(8,128)(2,1)S(1)} %collective-permute-done.2.refs_2_), channel_id=1, source_target_pairs={{0,2},{2,0},{4,6},{6,4},{8,10},{10,8},{12,14},{14,12},{16,18},{18,... | collective-permute-start | bytes 307208 | tf_op jit(solution)/shard_map/ppermute | solution.py:32
  17.0 2.4 %collective-permute-start.6 = (bf16[80,640]{1,0:T(8,128)(2,1)S(1)}, bf16[80,640]{1,0:T(8,128)(2,1)S(1)}, u32[]{:S(2)}, u32[]{:S(2)}) collective-permute-start(bf16[80,640]{1,0:T(8,128)(2,1)S(1)} %collective-permute-done.5.refs_4_), channel_id=1, source_target_pairs={{0,2},{2,0},{4,6},{6,4},{8,10},{10,8},{12,14},{14,12},{16,18},{18,... | collective-permute-start | bytes 307208 | tf_op jit(solution)/shard_map/ppermute | solution.py:32
  19.5 1.3 %collective-permute-start.12 = (bf16[80,640]{1,0:T(8,128)(2,1)S(1)}, bf16[80,640]{1,0:T(8,128)(2,1)S(1)}, u32[]{:S(2)}, u32[]{:S(2)}) collective-permute-start(bf16[80,640]{1,0:T(8,128)(2,1)S(1)} %collective-permute-done.11.refs_0_), channel_id=1, source_target_pairs={{0,2},{2,0},{4,6},{6,4},{8,10},{10,8},{12,14},{14,12},{16,18},{18,... | collective-permute-start | bytes 307208 | tf_op jit(solution)/shard_map/ppermute | solution.py:32
  21.1 5.0 %collective-permute-start.13 = (bf16[80,640]{1,0:T(8,128)(2,1)S(1)}, bf16[80,640]{1,0:T(8,128)(2,1)S(1)}, u32[]{:S(2)}, u32[]{:S(2)}) collective-permute-start(bf16[80,640]{1,0:T(8,128)(2,1)S(1)} %get-tuple-element.40.half), channel_id=1, source_target_pairs={{0,1},{1,0},{2,3},{3,2},{4,5},{5,4},{6,7},{7,6},{8,9},{9,8},{10,11... | collective-permute-start | bytes 307208 | tf_op jit(solution)/shard_map/ppermute | solution.py:171
where the time goes:
time: 27.2 us; the launch traced here: 27 us
  starting transfers between devices  15.3 us (56%)
  waiting for transfers between devices  7.31 us (27%)
  Pallas kernels  3.55 us (13%)
  other arithmetic  0.76 us (3%)
    ppermute x12, starting transfers between devices, send(): return lax.ppermute(value, 'grid', pairs)  12.2 us
    ppermute x12, waiting for transfers between devices, send(): return lax.ppermute(value, 'grid', pairs)  4.18 us
    pallas_call x7, Pallas kernels, call(): pl.pallas_call(kernel, out_shape=[jax.ShapeDtypeStruct(shape, dtype) for...  3.55 us
    ppermute x2, waiting for transfers between devices, shifted(): lax.ppermute(own, 'rep', [(s, (s + q) % reps) for s in range(reps)])  3.13 us
    ppermute x2, starting transfers between devices, shifted(): lax.ppermute(own, 'rep', [(s, (s + q) % reps) for s in range(reps)])  3.1 us
    concatenate x1, other arithmetic, on_device(): jnp.concatenate([density_pattern, square_pattern, cube_pattern, after(blo...  0.76 us
  transfers between devices with their start and end apart: 14, of which 4 were waited for; matrix products, arithmetic and copies ran while one was open for 3% of the time, Pallas kernels for 8%

commit v1 on v0

--- a/solution.py
+++ b/solution.py
@@ -223,18 +223,18 @@
         [panel_keep, after(density), *panel],
     )
 
-    lone = [(0, 0)] + [key for key in held if key[0] == last]
-    lone += [key for key in held if key[0] in before and key[1]]
-    stack = [key for key in held if key not in lone]
+    keys = [(0, 0)] + [(0, hop) for hop in hops] + [(step, 0) for step in steps]
+    keys += [(step, hop) for step in steps for hop in hops]
+    lone = [(0, 0)] + [key for key in keys if key[0] == last or key[0] in before and key[1]]
+    stack = [key for key in keys if key not in lone]
     whole = lambda key, core: (*key, core, 0, rows)
     early, late = [], []
-    for key in lone:
+    for key in keys:
         group = late if key[0] == last and key[1] else early
         group.append(([whole(key, 0)], held[key] if key != (0, 0) else own))
-        if pair > 1:
+        if pair > 1 and key in lone:
             value = after(held[key], *([] if group is late else [left]))
             group.append(([whole(key, 1)], send(value, dims, 2, 1)))
-    early += [([whole(key, 0)], held[key]) for key in stack]
     if pair > 1 and stack:
         ready = panel + ([held[last, 0]] if hops else [])
         (stacked,) = call(

time: 27.2 us -> 27.2 us (level)
  no operation moved by 1% of the time
where the time goes in v1:
time: 27.2 us; the launch traced here: 27 us
  starting transfers between devices  15.4 us (57%)
  waiting for transfers between devices  7.21 us (27%)
  Pallas kernels  3.55 us (13%)
  other arithmetic  0.76 us (3%)
    ppermute x12, starting transfers between devices, send(): return lax.ppermute(value, 'grid', pairs)  12.3 us
    ppermute x12, waiting for transfers between devices, send(): return lax.ppermute(value, 'grid', pairs)  4.06 us
    pallas_call x7, Pallas kernels, call(): pl.pallas_call(kernel, out_shape=[jax.ShapeDtypeStruct(shape, dtype) for...  3.55 us
    ppermute x2, waiting for transfers between devices, shifted(): lax.ppermute(own, 'rep', [(s, (s + q) % reps) for s in range(reps)])  3.15 us
    ppermute x2, starting transfers between devices, shifted(): lax.ppermute(own, 'rep', [(s, (s + q) % reps) for s in range(reps)])  3.09 us
    concatenate x1, other arithmetic, on_device(): jnp.concatenate([density_pattern, square_pattern, cube_pattern, after(blo...  0.76 us
  transfers between devices with their start and end apart: 14, of which 4 were waited for; matrix products, arithmetic and copies ran while one was open for 3% of the time, Pallas kernels for 8%

profile of v1, /device:TPU:0, one launch (start us, length us, event | category | flops | bytes accessed | tf_op | source)
XLA Modules:
  0.0 27.0 jit_solution(595270017192922474)
XLA Ops:
  0.0 3.0 %collective-permute-start.3 = (bf16[80,640]{1,0:T(8,128)(2,1)}, bf16[80,640]{1,0:T(8,128)(2,1)S(1)}, u32[]{:S(2)}, u32[]{:S(2)}) collective-permute-start(bf16[80,640]{1,0:T(8,128)(2,1)} %refs_0_), channel_id=1, source_target_pairs={{0,8},{2,10},{4,12},{6,14},{8,16},{10,18},{12,20},{14,22},{16,24},... | collective-permute-start | bytes 307208 | tf_op jit(solution)/shard_map/ppermute | solution.py:32
  3.0 2.0 %collective-permute-start.6 = (bf16[80,640]{1,0:T(8,128)(2,1)}, bf16[80,640]{1,0:T(8,128)(2,1)S(1)}, u32[]{:S(2)}, u32[]{:S(2)}) collective-permute-start(bf16[80,640]{1,0:T(8,128)(2,1)} %refs_0_), channel_id=1, source_target_pairs={{0,24},{2,26},{4,28},{6,30},{8,0},{10,2},{12,4},{14,6},{16,8},{18,... | collective-permute-start | bytes 307208 | tf_op jit(solution)/shard_map/ppermute | solution.py:32
  5.1 1.0 %collective-permute-start.4 = (bf16[80,640]{1,0:T(8,128)(2,1)}, bf16[80,640]{1,0:T(8,128)(2,1)S(1)}, u32[]{:S(2)}, u32[]{:S(2)}) collective-permute-start(bf16[80,640]{1,0:T(8,128)(2,1)} %refs_0_), channel_id=1, source_target_pairs={{0,16},{2,18},{4,20},{6,22},{8,24},{10,26},{12,28},{14,30},{16,0},... | collective-permute-start | bytes 307208 | tf_op jit(solution)/shard_map/ppermute | solution.py:32
  6.1 1.5 %collective-permute-start.2 = (bf16[80,640]{1,0:T(8,128)(2,1)}, bf16[80,640]{1,0:T(8,128)(2,1)S(1)}, u32[]{:S(2)}, u32[]{:S(2)}) collective-permute-start(bf16[80,640]{1,0:T(8,128)(2,1)} %refs_0_), channel_id=1, source_target_pairs={{0,4},{2,6},{4,0},{6,2},{8,12},{10,14},{12,8},{14,10},{16,20},{18,... | collective-permute-start | bytes 307208 | tf_op jit(solution)/shard_map/ppermute | solution.py:32
  7.6 1.5 %collective-permute-start = (bf16[80,640]{1,0:T(8,128)(2,1)}, bf16[80,640]{1,0:T(8,128)(2,1)S(1)}, u32[]{:S(2)}, u32[]{:S(2)}) collective-permute-start(bf16[80,640]{1,0:T(8,128)(2,1)} %refs_0_), channel_id=1, source_target_pairs={{0,1},{1,0},{2,3},{3,2},{4,5},{5,4},{6,7},{7,6},{8,9},{9,8},{10,11... | collective-permute-start | bytes 307208 | tf_op jit(solution)/shard_map/ppermute | solution.py:171
  9.1 0.0 collective-permute-done.3.refs_1_.refs_3_
  9.1 1.4 %collective-permute-start.7 = (bf16[80,640]{1,0:T(8,128)(2,1)S(1)}, bf16[80,640]{1,0:T(8,128)(2,1)S(1)}, u32[]{:S(2)}, u32[]{:S(2)}) collective-permute-start(bf16[80,640]{1,0:T(8,128)(2,1)S(1)} %collective-permute-done.3.refs_1_.refs_3_), channel_id=1, source_target_pairs={{0,4},{2,6},{4,0},{6,2},{8,12},{10,14},{12,8},{14,10},{16,20},{18,... | collective-permute-start | bytes 307208 | tf_op jit(solution)/shard_map/ppermute | solution.py:32
  10.5 0.8 %pad_add_fusion.packed = s32[31,10]{1,0:T(8,128)S(1)} fusion(s32[1,10]{1,0:T(1,128)} %bitcast.1, s32[10,10]{1,0:T(8,128)} %param.8, s32[10,10]{1,0:T(8,128)} %param.7, s32[10,10]{1,0:T(8,128)} %param.6), kind=kLoop, calls=%fused_computation | loop fusion | flops 930 | bytes 2480 | tf_op jit(solution)/shard_map/concatenate | solution.py:206
  11.2 0.0 copy-start
  11.2 1.0 %prepare.1 = (bf16[10,16,640]{2,1,0:T(8,128)(2,1)S(1)}, bf16[2,80,640]{2,1,0:T(8,128)(2,1)S(1)}, f32[80,640]{1,0:T(8,128)S(1)}, f32[80,640]{1,0:T(8,128)S(1)}) custom-call(s32[31,10]{1,0:T(8,128)S(1)} %pad_add_fusion.packed), custom_call_target="tpu_custom_call" | custom-call | flops 1000000000 | bytes 3276800 | tf_op jit(solution)/shard_map/prepare/pallas_call | solution.py:186
  12.3 0.0 collective-permute-done.6.refs_2_.refs_6_
  12.3 0.7 %collective-permute-start.8 = (bf16[80,640]{1,0:T(8,128)(2,1)S(1)}, bf16[80,640]{1,0:T(8,128)(2,1)S(1)}, u32[]{:S(2)}, u32[]{:S(2)}) collective-permute-start(bf16[80,640]{1,0:T(8,128)(2,1)S(1)} %collective-permute-done.6.refs_2_.refs_6_), channel_id=1, source_target_pairs={{0,4},{2,6},{4,0},{6,2},{8,12},{10,14},{12,8},{14,10},{16,20},{18,... | collective-permute-start | bytes 307208 | tf_op jit(solution)/shard_map/ppermute | solution.py:32
  13.0 1.7 %collective-permute-done.4.refs_4_ = bf16[80,640]{1,0:T(8,128)(2,1)S(1)} collective-permute-done((bf16[80,640]{1,0:T(8,128)(2,1)}, bf16[80,640]{1,0:T(8,128)(2,1)S(1)}, u32[]{:S(2)}, u32[]{:S(2)}) %collective-permute-start.4) | collective-permute-done | bytes 102432 | tf_op jit(solution)/shard_map/ppermute | solution.py:32
  14.7 0.0 collective-permute-done.refs_1_
  14.7 0.0 collective-permute-done.2.refs_0_.refs_2_
  14.7 1.5 %collective-permute-start.11 = (bf16[80,640]{1,0:T(8,128)(2,1)S(1)}, bf16[80,640]{1,0:T(8,128)(2,1)S(1)}, u32[]{:S(2)}, u32[]{:S(2)}) collective-permute-start(bf16[80,640]{1,0:T(8,128)(2,1)S(1)} %collective-permute-done.4.refs_4_), channel_id=1, source_target_pairs={{0,4},{2,6},{4,0},{6,2},{8,12},{10,14},{12,8},{14,10},{16,20},{18,... | collective-permute-start | bytes 307208 | tf_op jit(solution)/shard_map/ppermute | solution.py:32
  16.2 0.0 collective-permute-done.7.refs_3_.refs_7_
  16.3 0.1 collective-permute-start.10
  16.3 0.0 copy-done
  16.4 0.6 %collective-permute-start.1 = (bf16[80,640]{1,0:T(8,128)(2,1)S(1)}, bf16[80,640]{1,0:T(8,128)(2,1)S(1)}, u32[]{:S(2)}, u32[]{:S(2)}) collective-permute-start(bf16[80,640]{1,0:T(8,128)(2,1)S(1)} %copy-done), channel_id=1, source_target_pairs={{0,2},{2,0},{4,6},{6,4},{8,10},{10,8},{12,14},{14,12},{16,18},{18,... | collective-permute-start | bytes 307208 | tf_op jit(solution)/shard_map/ppermute | solution.py:32
  17.0 0.1 collective-permute-start.5
  17.0 0.0 collective-permute-done.8.refs_8_
  17.0 0.4 %collective-permute-start.9 = (bf16[80,640]{1,0:T(8,128)(2,1)S(1)}, bf16[80,640]{1,0:T(8,128)(2,1)S(1)}, u32[]{:S(2)}, u32[]{:S(2)}) collective-permute-start(bf16[80,640]{1,0:T(8,128)(2,1)S(1)} %collective-permute-done.8.refs_8_), channel_id=1, source_target_pairs={{0,2},{2,0},{4,6},{6,4},{8,10},{10,8},{12,14},{14,12},{16,18},{18,... | collective-permute-start | bytes 307208 | tf_op jit(solution)/shard_map/ppermute | solution.py:32
  17.5 1.9 %collective-permute-done.11.refs_0_ = bf16[80,640]{1,0:T(8,128)(2,1)S(1)} collective-permute-done((bf16[80,640]{1,0:T(8,128)(2,1)S(1)}, bf16[80,640]{1,0:T(8,128)(2,1)S(1)}, u32[]{:S(2)}, u32[]{:S(2)}) %collective-permute-start.11) | collective-permute-done | bytes 102432 | tf_op jit(solution)/shard_map/ppermute | solution.py:32
  19.4 0.0 collective-permute-start.12
  19.4 0.0 collective-permute-done.1.refs_1_
  19.4 0.0 collective-permute-done.5.refs_5_
  19.4 0.0 collective-permute-done.9.refs_9_
  19.4 0.0 collective-permute-done.10.refs_10_
  19.4 0.9 %square_early.1 = (bf16[1280,640]{1,0:T(8,128)(2,1)S(1)}, f32[80,640]{1,0:T(8,128)S(1)}) custom-call(bf16[80,1280]{1,0:T(8,128)(2,1)S(1)} %get-tuple-element.28.left, bf16[10,16,640]{2,1,0:T(8,128)(2,1)S(1)} %get-tuple-element.25.table, bf16[80,640]{1,0:T(8,128)(2,1)S(1)} %get-tuple-element.29.refs_0_, bf16[80,640]{1,0:T(8,128)(2,1)S(1)} %collective-permute-done.1.refs_1_, ...), custom_call_target="tpu_custom_call" | custom-call | flops 131072000 | bytes 3276800 | tf_op jit(solution)/shard_map/square_early/pallas_call | solution.py:186
  20.3 0.4 %collective-permute-done.12.refs_1_ = bf16[80,640]{1,0:T(8,128)(2,1)S(1)} collective-permute-done((bf16[80,640]{1,0:T(8,128)(2,1)S(1)}, bf16[80,640]{1,0:T(8,128)(2,1)S(1)}, u32[]{:S(2)}, u32[]{:S(2)}) %collective-permute-start.12) | collective-permute-done | bytes 102432 | tf_op jit(solution)/shard_map/ppermute | solution.py:32
  20.7 0.3 %square_late.1 = (bf16[1280,640]{1,0:T(8,128)(2,1)S(1)}, f32[80,640]{1,0:T(8,128)S(1)}, bf16[80,640]{1,0:T(8,128)(2,1)S(1)}) custom-call(bf16[10,16,640]{2,1,0:T(8,128)(2,1)S(1)} %get-tuple-element.25.table, f32[80,640]{1,0:T(8,128)S(1)} %get-tuple-element.26.square_keep, ...), custom_call_target="tpu_custom_call", output_to_operand_aliasing={{0}: (3, {})} | custom-call | flops 26214400 | bytes 204800 | tf_op jit(solution)/shard_map/square_late/pallas_call | solution.py:186
  21.0 1.6 %collective-permute-start.13 = (bf16[80,640]{1,0:T(8,128)(2,1)S(1)}, bf16[80,640]{1,0:T(8,128)(2,1)S(1)}, u32[]{:S(2)}, u32[]{:S(2)}) collective-permute-start(bf16[80,640]{1,0:T(8,128)(2,1)S(1)} %get-tuple-element.40.half), channel_id=1, source_target_pairs={{0,1},{1,0},{2,3},{3,2},{4,5},{5,4},{6,7},{7,6},{8,9},{9,8},{10,11... | collective-permute-start | bytes 307208 | tf_op jit(solution)/shard_map/ppermute | solution.py:171
  22.6 0.3 %cube_part.2.before = f32[80,640]{1,0:T(8,128)S(1)} custom-call(f32[80,640]{1,0:T(8,128)S(1)} %get-tuple-element.24.keep, bf16[80,640]{1,0:T(8,128)(2,1)S(1)} %get-tuple-element.40.half, bf16[1280,640]{1,0:T(8,128)(2,1)S(1)} %get-tuple-element.41.band, f32[80,640]{1,0:T(8,128)S(1)} %get-tuple-element.42.before), custom_call_target="tpu_custom_call" | custom-call | flops 65536000 | bytes 819200 | tf_op jit(solution)/shard_map/cube_part/pallas_call | solution.py:186
  22.9 3.1 %collective-permute-done.13.half = bf16[80,640]{1,0:T(8,128)(2,1)S(1)} collective-permute-done((bf16[80,640]{1,0:T(8,128)(2,1)S(1)}, bf16[80,640]{1,0:T(8,128)(2,1)S(1)}, u32[]{:S(2)}, u32[]{:S(2)}) %collective-permute-start.13) | collective-permute-done | bytes 102432 | tf_op jit(solution)/shard_map/ppermute | solution.py:171
  26.0 1.0 %cube_part.3 = f32[80,640]{1,0:T(8,128)} custom-call(f32[80,640]{1,0:T(8,128)S(1)} %get-tuple-element.24.keep, bf16[80,640]{1,0:T(8,128)(2,1)S(1)} %collective-permute-done.13.half, bf16[1280,640]{1,0:T(8,128)(2,1)S(1)} %get-tuple-element.41.band, f32[80,640]{1,0:T(8,128)S(1)} %cube_part.2.before), custom_call_target="tpu_custom_call" | custom-call | flops 65536000 | bytes 819200 | tf_op jit(solution)/shard_map/cube_part/pallas_call | solution.py:186
  (2 shorter events, 0.1 us)
Async XLA Ops:
  0.0 9.1 %collective-permute-start.3 = (bf16[80,640]{1,0:T(8,128)(2,1)}, bf16[80,640]{1,0:T(8,128)(2,1)S(1)}, u32[]{:S(2)}, u32[]{:S(2)}) collective-permute-start(bf16[80,640]{1,0:T(8,128)(2,1)} %refs_0_), channel_id=1, source_target_pairs={{0,8},{2,10},{4,12},{6,14},{8,16},{10,18},{12,20},{14,22},{16,24},... | collective-permute-start | bytes 307208 | tf_op jit(solution)/shard_map/ppermute | solution.py:32
  3.0 9.2 %collective-permute-start.6 = (bf16[80,640]{1,0:T(8,128)(2,1)}, bf16[80,640]{1,0:T(8,128)(2,1)S(1)}, u32[]{:S(2)}, u32[]{:S(2)}) collective-permute-start(bf16[80,640]{1,0:T(8,128)(2,1)} %refs_0_), channel_id=1, source_target_pairs={{0,24},{2,26},{4,28},{6,30},{8,0},{10,2},{12,4},{14,6},{16,8},{18,... | collective-permute-start | bytes 307208 | tf_op jit(solution)/shard_map/ppermute | solution.py:32
  5.1 9.7 %collective-permute-start.4 = (bf16[80,640]{1,0:T(8,128)(2,1)}, bf16[80,640]{1,0:T(8,128)(2,1)S(1)}, u32[]{:S(2)}, u32[]{:S(2)}) collective-permute-start(bf16[80,640]{1,0:T(8,128)(2,1)} %refs_0_), channel_id=1, source_target_pairs={{0,16},{2,18},{4,20},{6,22},{8,24},{10,26},{12,28},{14,30},{16,0},... | collective-permute-start | bytes 307208 | tf_op jit(solution)/shard_map/ppermute | solution.py:32
  6.1 8.7 %collective-permute-start.2 = (bf16[80,640]{1,0:T(8,128)(2,1)}, bf16[80,640]{1,0:T(8,128)(2,1)S(1)}, u32[]{:S(2)}, u32[]{:S(2)}) collective-permute-start(bf16[80,640]{1,0:T(8,128)(2,1)} %refs_0_), channel_id=1, source_target_pairs={{0,4},{2,6},{4,0},{6,2},{8,12},{10,14},{12,8},{14,10},{16,20},{18,... | collective-permute-start | bytes 307208 | tf_op jit(solution)/shard_map/ppermute | solution.py:32
  7.6 7.2 %collective-permute-start = (bf16[80,640]{1,0:T(8,128)(2,1)}, bf16[80,640]{1,0:T(8,128)(2,1)S(1)}, u32[]{:S(2)}, u32[]{:S(2)}) collective-permute-start(bf16[80,640]{1,0:T(8,128)(2,1)} %refs_0_), channel_id=1, source_target_pairs={{0,1},{1,0},{2,3},{3,2},{4,5},{5,4},{6,7},{7,6},{8,9},{9,8},{10,11... | collective-permute-start | bytes 307208 | tf_op jit(solution)/shard_map/ppermute | solution.py:171
  9.1 7.1 %collective-permute-start.7 = (bf16[80,640]{1,0:T(8,128)(2,1)S(1)}, bf16[80,640]{1,0:T(8,128)(2,1)S(1)}, u32[]{:S(2)}, u32[]{:S(2)}) collective-permute-start(bf16[80,640]{1,0:T(8,128)(2,1)S(1)} %collective-permute-done.3.refs_1_.refs_3_), channel_id=1, source_target_pairs={{0,4},{2,6},{4,0},{6,2},{8,12},{10,14},{12,8},{14,10},{16,20},{18,... | collective-permute-start | bytes 307208 | tf_op jit(solution)/shard_map/ppermute | solution.py:32
  11.2 5.1 %copy-start = (bf16[80,640]{1,0:T(8,128)(2,1)S(1)}, bf16[80,640]{1,0:T(8,128)(2,1)}, u32[]{:S(2)}) copy-start(bf16[80,640]{1,0:T(8,128)(2,1)} %refs_0_) | copy-start | bytes 307204
  12.3 4.8 %collective-permute-start.8 = (bf16[80,640]{1,0:T(8,128)(2,1)S(1)}, bf16[80,640]{1,0:T(8,128)(2,1)S(1)}, u32[]{:S(2)}, u32[]{:S(2)}) collective-permute-start(bf16[80,640]{1,0:T(8,128)(2,1)S(1)} %collective-permute-done.6.refs_2_.refs_6_), channel_id=1, source_target_pairs={{0,4},{2,6},{4,0},{6,2},{8,12},{10,14},{12,8},{14,10},{16,20},{18,... | collective-permute-start | bytes 307208 | tf_op jit(solution)/shard_map/ppermute | solution.py:32
  14.7 4.7 %collective-permute-start.11 = (bf16[80,640]{1,0:T(8,128)(2,1)S(1)}, bf16[80,640]{1,0:T(8,128)(2,1)S(1)}, u32[]{:S(2)}, u32[]{:S(2)}) collective-permute-start(bf16[80,640]{1,0:T(8,128)(2,1)S(1)} %collective-permute-done.4.refs_4_), channel_id=1, source_target_pairs={{0,4},{2,6},{4,0},{6,2},{8,12},{10,14},{12,8},{14,10},{16,20},{18,... | collective-permute-start | bytes 307208 | tf_op jit(solution)/shard_map/ppermute | solution.py:32
  16.3 3.2 %collective-permute-start.10 = (bf16[320,640]{1,0:T(8,128)(2,1)S(1)}, bf16[320,640]{1,0:T(8,128)(2,1)S(1)}, u32[]{:S(2)}, u32[]{:S(2)}) collective-permute-start(bf16[320,640]{1,0:T(8,128)(2,1)S(1)} %stack.1), channel_id=1, source_target_pairs={{0,2},{2,0},{4,6},{6,4},{8,10},{10,8},{12,14},{14,12},{16,18},{18,... | collective-permute-start | bytes 1228808 | tf_op jit(solution)/shard_map/ppermute | solution.py:32
  16.4 3.0 %collective-permute-start.1 = (bf16[80,640]{1,0:T(8,128)(2,1)S(1)}, bf16[80,640]{1,0:T(8,128)(2,1)S(1)}, u32[]{:S(2)}, u32[]{:S(2)}) collective-permute-start(bf16[80,640]{1,0:T(8,128)(2,1)S(1)} %copy-done), channel_id=1, source_target_pairs={{0,2},{2,0},{4,6},{6,4},{8,10},{10,8},{12,14},{14,12},{16,18},{18,... | collective-permute-start | bytes 307208 | tf_op jit(solution)/shard_map/ppermute | solution.py:32
  17.0 2.5 %collective-permute-start.5 = (bf16[80,640]{1,0:T(8,128)(2,1)S(1)}, bf16[80,640]{1,0:T(8,128)(2,1)S(1)}, u32[]{:S(2)}, u32[]{:S(2)}) collective-permute-start(bf16[80,640]{1,0:T(8,128)(2,1)S(1)} %collective-permute-done.4.refs_4_), channel_id=1, source_target_pairs={{0,2},{2,0},{4,6},{6,4},{8,10},{10,8},{12,14},{14,12},{16,18},{18,... | collective-permute-start | bytes 307208 | tf_op jit(solution)/shard_map/ppermute | solution.py:32
  17.0 2.4 %collective-permute-start.9 = (bf16[80,640]{1,0:T(8,128)(2,1)S(1)}, bf16[80,640]{1,0:T(8,128)(2,1)S(1)}, u32[]{:S(2)}, u32[]{:S(2)}) collective-permute-start(bf16[80,640]{1,0:T(8,128)(2,1)S(1)} %collective-permute-done.8.refs_8_), channel_id=1, source_target_pairs={{0,2},{2,0},{4,6},{6,4},{8,10},{10,8},{12,14},{14,12},{16,18},{18,... | collective-permute-start | bytes 307208 | tf_op jit(solution)/shard_map/ppermute | solution.py:32
  19.4 1.3 %collective-permute-start.12 = (bf16[80,640]{1,0:T(8,128)(2,1)S(1)}, bf16[80,640]{1,0:T(8,128)(2,1)S(1)}, u32[]{:S(2)}, u32[]{:S(2)}) collective-permute-start(bf16[80,640]{1,0:T(8,128)(2,1)S(1)} %collective-permute-done.11.refs_0_), channel_id=1, source_target_pairs={{0,2},{2,0},{4,6},{6,4},{8,10},{10,8},{12,14},{14,12},{16,18},{18,... | collective-permute-start | bytes 307208 | tf_op jit(solution)/shard_map/ppermute | solution.py:32
  21.0 5.0 %collective-permute-start.13 = (bf16[80,640]{1,0:T(8,128)(2,1)S(1)}, bf16[80,640]{1,0:T(8,128)(2,1)S(1)}, u32[]{:S(2)}, u32[]{:S(2)}) collective-permute-start(bf16[80,640]{1,0:T(8,128)(2,1)S(1)} %get-tuple-element.40.half), channel_id=1, source_target_pairs={{0,1},{1,0},{2,3},{3,2},{4,5},{5,4},{6,7},{7,6},{8,9},{9,8},{10,11... | collective-permute-start | bytes 307208 | tf_op jit(solution)/shard_map/ppermute | solution.py:171
